TPU v7x, 256 devices: a whole 4x4x8 slice. The times are simulated.
256 devices in a mesh: grp: 8 (over z), voc: 32 (over y, x, core).
Axes of the slice: x: 4, y: 4, z: 8, core: 2. Of those that a mesh axis runs over, the one named last changes fastest.
Arguments:
- hidden: bfloat16 [2048, 1280], P(('grp', 'voc')), parts along dimension 0, may hold values from -16 to 16
- head_weight: bfloat16 [1280, 77824], P(None, 'voc'), may hold values from -3 to 3
- teacher_logits: bfloat16 [2048, 77824], P(('grp', 'voc')), parts along dimension 0, may hold values from -18 to 360
- token_ids: int32 [2048], P('grp'), parts along dimension 0, may hold values from 0 to 77823
- teacher_map: int32 [32], replicated, may hold values from 0 to 31, each once
- student_map: int32 [32], replicated, may hold values from 0 to 31, each once
Outputs:
- divergence: float32 [2048], P('grp'), parts along dimension 0
- hidden_grad: bfloat16 [2048, 1280], P(('grp', 'voc')), parts along dimension 0
- weight_grad: bfloat16 [1280, 622592], P(None, ('grp', 'voc')), parts along dimension 1
There are 8 independent parts, one for each index of `grp`. A program takes and returns all parts, laid end to end along the dimension named above; an argument that names none is the same for every part. Nothing has to cross between parts.
Inputs may be any that keep to these rules, and one draw needn't show every extreme that they name: `teacher_map`: a permutation of the 32 blocks. `student_map`: a permutation of the 32 blocks.
All inputs are finite; a program needn't handle non-finite values.
Results may differ from a plain program's by a relative error of at most 0.0053.
Values may be sent and summed in bfloat16 or wider, within the bound.
A program may use at most 64 MiB of HBM per device.

v0:
```python
import jax
import jax.numpy as jnp
from jax import lax
from jax.sharding import PartitionSpec as P


def on_device(hidden, head_weight, teacher_logits, token_ids, teacher_map, student_map):
    blocks = lax.axis_size("voc")
    own_index = lax.axis_index("voc")
    block_width = head_weight.shape[1]
    tok_local = hidden.shape[0]
    matches = (teacher_map[:, None] == student_map[None, :]).astype(jnp.int32)
    positions = jnp.sum(matches * jnp.arange(blocks, dtype=jnp.int32)[:, None], axis=0)
    ordered = jnp.take(teacher_logits.reshape(tok_local, blocks, block_width), positions, axis=1)
    ordered = ordered.reshape(tok_local, blocks * block_width)
    teacher_block = lax.all_to_all(ordered, "voc", split_axis=1, concat_axis=0, tiled=True)
    all_hidden = lax.all_gather(hidden, "voc", axis=0, tiled=True)
    logits = jnp.dot(all_hidden, head_weight, preferred_element_type=jnp.float32)
    teacher = teacher_block.astype(jnp.float32)
    owned_block = jnp.take(student_map, own_index)
    column_ids = owned_block * block_width + jnp.arange(block_width, dtype=jnp.int32)
    sampled_mask = column_ids[None, :] == token_ids[:, None]
    top_student, top_teacher = lax.pmax((jnp.max(logits, axis=1), jnp.max(teacher, axis=1)), "voc")
    total_student, total_teacher = lax.psum(
        (
            jnp.sum(jnp.exp(logits - top_student[:, None]), axis=1),
            jnp.sum(jnp.exp(teacher - top_teacher[:, None]), axis=1),
        ),
        "voc",
    )
    norm_student = top_student + jnp.log(total_student)
    norm_teacher = top_teacher + jnp.log(total_teacher)
    log_student = logits - norm_student[:, None]
    log_teacher = teacher - norm_teacher[:, None]
    student_prob = jnp.exp(log_student)
    gap = log_student - log_teacher
    divergence, sampled_gap = lax.psum(
        (jnp.sum(student_prob * gap, axis=1), jnp.sum(jnp.where(sampled_mask, gap, 0.0), axis=1)),
        "voc",
    )
    logit_grad = student_prob * (gap - divergence[:, None]) + sampled_gap[:, None] * (
        sampled_mask.astype(jnp.float32) - student_prob
    )
    logit_grad = logit_grad.astype(jnp.bfloat16)
    weight_grad = lax.dot_general(
        all_hidden, logit_grad, (((0,), (0,)), ((), ())), preferred_element_type=jnp.float32
    ).astype(jnp.bfloat16)
    summed_grad = lax.psum(
        lax.dot_general(
            logit_grad, head_weight, (((1,), (1,)), ((), ())), preferred_element_type=jnp.float32
        ),
        "voc",
    )
    hidden_grad = lax.dynamic_slice_in_dim(summed_grad, own_index * tok_local, tok_local, 0).astype(
        jnp.bfloat16
    )
    return (divergence, hidden_grad, weight_grad)


def solution(mesh):
    return jax.shard_map(
        on_device,
        mesh=mesh,
        in_specs=(
            P(("grp", "voc"), None),
            P(None, "voc"),
            P(("grp", "voc"), None),
            P("grp"),
            P(),
            P(),
        ),
        out_specs=(P("grp"), P(("grp", "voc"), None), P(None, ("grp", "voc"))),
        check_vma=False,
    )
```

profile of v0, /device:TPU:1, one launch (start us, length us, event | category | flops | bytes accessed | tf_op | source)
XLA Modules:
  0.0 405.8 jit_solution(13071723295383985819)
XLA Ops:
  0.6 0.9 select_reduce_fusion
  1.5 0.4 copy-done
  2.0 0.7 gather_fusion
  2.7 1.2 select_bitcast_fusion
  4.0 8.6 %all-to-all-start = ((bf16[8,32,2432]{2,0,1:T(8,128)(2,1)}), bf16[8,32,2432]{2,0,1:T(8,128)(2,1)S(1)}, u32[]{:S(2)}, u32[]{:S(2)}) async-start(bf16[8,32,2432]{2,0,1:T(8,128)(2,1)} %select_bitcast_fusion), calls=%async_computation | async-start | bytes 2490368 | tf_op jit(solution)/shard_map/all_to_all | solution.py:16
  12.6 0.6 dynamic-slice.2
  13.8 33.9 %all_gather.3 = bf16[256,1280]{1,0:T(8,128)(2,1)S(1)} all-gather(bf16[8,1280]{1,0:T(8,128)(2,1)S(1)} %copy-done.1), channel_id=1, replica_groups=mesh['grp'=8,'voc'=32] {'voc'}, dimensions={0}, use_global_device_ids=true | all-gather | bytes 675840 | tf_op jit(solution)/shard_map/all_gather | solution.py:17
  47.7 6.1 %fusion.11 = (f32[256]{0:T(256)S(1)}, f32[256,2432]{1,0:T(8,128)}) fusion(bf16[256,1280]{1,0:T(8,128)(2,1)S(1)} %all_gather.3, bf16[1280,2432]{1,0:T(8,128)(2,1)} %param.7), kind=kOutput, calls=%fused_computation.30 | convolution fusion | flops 1594457856 | bytes 9372672 | tf_op jit(solution)/shard_map/dot_general | solution.py:18
  53.8 0.3 bitcast_reduce_fusion
  54.1 0.1 reshape.86
  54.2 62.2 %all-reduce.2 = (f32[256]{0:T(256)S(1)}, f32[256]{0:T(256)S(1)}) all-reduce(f32[256]{0:T(256)S(1)} %reshape.86, f32[256]{0:T(256)S(1)} %get-tuple-element.31), channel_id=1, replica_groups=mesh['grp'=8,'voc'=32] {'voc'}, use_global_device_ids=true, to_apply=%region_6.7 | all-reduce | flops 512 | bytes 4096 | tf_op jit(solution)/shard_map/pmax | solution.py:23
  116.3 0.1 sub.53
  116.4 0.6 fusion.4
  117.0 0.1 reduce_sum.53
  117.1 2.2 exponential_reduce_fusion
  119.3 65.3 %all-reduce.1 = (f32[256]{0:T(256)S(1)}, f32[256]{0:T(256)S(1)}) all-reduce(f32[256]{0:T(256)S(1)} %reduce_sum.53, f32[256]{0:T(256)S(1)} %exponential_reduce_fusion), channel_id=1, replica_groups=mesh['grp'=8,'voc'=32] {'voc'}, use_global_device_ids=true, to_apply=%region_8.9 | all-reduce | flops 512 | bytes 4096 | tf_op jit(solution)/shard_map/psum | solution.py:24
  184.6 2.8 fusion.5
  187.4 62.7 %all-reduce = (f32[256]{0:T(256)S(1)}, f32[256]{0:T(256)S(1)}) all-reduce(f32[256]{0:T(256)S(1)} %get-tuple-element.24, f32[256]{0:T(256)S(1)} %get-tuple-element.23), channel_id=1, replica_groups=mesh['grp'=8,'voc'=32] {'voc'}, use_global_device_ids=true, to_apply=%region_10.11 | all-reduce | flops 512 | bytes 4096 | tf_op jit(solution)/shard_map/psum | solution.py:37
  250.1 3.2 fusion.9
  253.3 5.7 %fusion.12 = f32[256,1280]{1,0:T(8,128)} fusion(bf16[256,2432]{1,0:T(8,128)(2,1)S(1)} %fusion.9, bf16[1280,2432]{1,0:T(8,128)(2,1)} %param.7), kind=kOutput, calls=%fused_computation.31 | convolution fusion | flops 1593835520 | bytes 8781824 | tf_op jit(solution)/shard_map/dot_general | solution.py:49
  259.0 4.5 %fusion = bf16[1280,2432]{0,1:T(8,128)(2,1)} fusion(bf16[256,2432]{1,0:T(8,128)(2,1)S(1)} %fusion.9, bf16[256,1280]{1,0:T(8,128)(2,1)S(1)} %all_gather.3), kind=kOutput, calls=%fused_computation.2 | convolution fusion | flops 1596948480 | bytes 8126464 | tf_op jit(solution)/shard_map/dot_general | solution.py:45
  263.5 132.3 %all-reduce.4 = bf16[256,1280]{1,0:T(8,128)(2,1)S(1)} all-reduce(f32[256,1280]{1,0:T(8,128)} %fusion.12), channel_id=1, replica_groups=mesh['grp'=8,'voc'=32] {'voc'}, use_global_device_ids=true, to_apply=%region_13.14 | all-reduce | flops 327680 | bytes 1966080 | tf_op jit(solution)/shard_map/psum | solution.py:48
  395.8 9.3 %copy.11 = bf16[1280,2432]{1,0:T(8,128)(2,1)} copy(bf16[1280,2432]{0,1:T(8,128)(2,1)} %fusion) | data formatting | bytes 12451840
  405.1 0.6 dynamic-slice_convert_fusion
  (15 shorter events, 0.1 us)
Async XLA Ops:
  0.6 1.3 copy-start
  2.7 9.9 %copy-start.4 = (s32[32]{0:T(128)S(1)}, s32[32]{0:T(128)}, u32[]{:S(2)}) copy-start(s32[32]{0:T(128)} %param.11) | copy-start | bytes 388
  2.7 11.1 %copy-start.1 = (bf16[8,1280]{1,0:T(8,128)(2,1)S(1)}, bf16[8,1280]{1,0:T(8,128)(2,1)}, u32[]{:S(2)}) copy-start(bf16[8,1280]{1,0:T(8,128)(2,1)} %param.6) | copy-start | bytes 61444
  4.0 49.8 %all-to-all-start = ((bf16[8,32,2432]{2,0,1:T(8,128)(2,1)}), bf16[8,32,2432]{2,0,1:T(8,128)(2,1)S(1)}, u32[]{:S(2)}, u32[]{:S(2)}) async-start(bf16[8,32,2432]{2,0,1:T(8,128)(2,1)} %select_bitcast_fusion), calls=%async_computation | async-start | bytes 2490368 | tf_op jit(solution)/shard_map/all_to_all | solution.py:16
  53.8 130.8 %copy-start.2 = (s32[256]{0:T(256)S(1)}, s32[256]{0:T(256)}, u32[]{:S(2)}) copy-start(s32[256]{0:T(256)} %param.9) | copy-start | bytes 3076
  250.1 3.2 copy-start.3
where the time goes:
time: 411 us; the launch traced here: 406 us
  blocking collectives  356 us (87%)
  matrix products  16.3 us (4%)
  local copies, waits for them, and re-layouts  11.9 us (3%)
  other arithmetic  11.2 us (3%)
  starting transfers between devices  8.59 us (2%)
    psum x1, blocking collectives, on_device(): lax.psum(lax.dot_general(logit_grad, head_weight, (((1,), (1,)), ((), ())...  132 us
    psum x1, blocking collectives, on_device(): lax.psum((jnp.sum(jnp.exp(logits - top_student[:, None]), axis=1), jnp.su...  65.3 us
    psum x1, blocking collectives, on_device(): lax.psum((jnp.sum(student_prob * gap, axis=1), jnp.sum(jnp.where(sampled_...  62.7 us
    pmax x1, blocking collectives, on_device(): lax.pmax((jnp.max(logits, axis=1), jnp.max(teacher, axis=1)), 'voc')  62.2 us
    all_gather x1, blocking collectives, on_device(): all_hidden = lax.all_gather(hidden, 'voc', axis=0, tiled=True)  33.9 us
    unnamed x11, local copies, waits for them, and re-layouts  9.76 us
    all_to_all x1, starting transfers between devices, on_device(): lax.all_to_all(ordered, 'voc', split_axis=1, concat_axis=0, tiled=True)  8.59 us
  transfers between devices with their start and end apart: 1, of which 0 were waited for; matrix products, arithmetic and copies ran while one was open for 2% of the time, Pallas kernels for 0%

commit v1 on v0

v1 whole, which is shorter than its diff:
```python
import functools

import jax
import jax.numpy as jnp
from jax import lax
from jax.experimental import pallas as pl
from jax.experimental.pallas import tpu as pltpu
from jax.sharding import PartitionSpec as P

MESH = pl.DeviceIdType.MESH
F32 = jnp.float32
BF16 = jnp.bfloat16


def tiles(width, size):
    return [(start, min(size, width - start)) for start in range(0, width, size)]


def kernel(
    n,
    hidden_ref,
    head_ref,
    teacher_ref,
    token_ref,
    teacher_map,
    student_map,
    div_ref,
    hgrad_ref,
    wgrad_ref,
    head,
    mine,
    staged,
    teacher,
    gathered,
    hid,
    hid_t,
    diff,
    expo,
    grad,
    tok_col,
    stat,
    stat_out,
    stat_in,
    part_sib,
    part_own,
    pair_in,
    red_out,
    red_in,
    local_sem,
    m_sem,
    t_send,
    t_recv,
    h_send,
    h_recv,
    f_send,
    f_recv,
    s_send,
    s_recv,
    p_send,
    p_recv,
    r_send,
    r_recv,
):
    chips = n // 2
    rows, width = hidden_ref.shape
    block = head_ref.shape[1]
    half = chips * rows
    tokens = 2 * half
    me = lax.axis_index("voc")
    core, chip = me % 2, me // 2
    sibling = me + 1 - 2 * core
    my_block = core * chips + chip

    def slot(device):
        return (device % 2) * chips + device // 2

    def remote(src, dst, send, recv, device):
        return pltpu.make_async_remote_copy(
            src_ref=src, dst_ref=dst, send_sem=send, recv_sem=recv,
            device_id={"voc": device}, device_id_type=MESH,
        )

    barrier = pltpu.get_barrier_semaphore()

    @pl.loop(1, n)
    def _(step):
        pl.semaphore_signal(barrier, inc=1, device_id={"voc": (me + step) % n}, device_id_type=MESH)

    def teacher_in(p):
        return pltpu.make_async_copy(
            teacher_ref.at[:, pl.ds(pl.multiple_of(p * block, 128), block)], mine.at[p], m_sem.at[p]
        )

    @pl.loop(0, n)
    def _(p):
        teacher_in(p).start()

    head_in = pltpu.make_async_copy(head_ref, head, local_sem.at[0])
    head_in.start()

    eye = (
        lax.broadcasted_iota(jnp.int32, (tokens, tokens), 0)
        == lax.broadcasted_iota(jnp.int32, (tokens, tokens), 1)
    )
    ids = jnp.sum(jnp.where(eye, token_ref[...].astype(F32), 0.0), axis=1, keepdims=True)
    ids = ids - (student_map[me] * block).astype(F32)
    ids = jnp.broadcast_to(ids, (tokens, 128)).reshape(chips, 2, rows, 128)
    tok_col[...] = jnp.concatenate([ids[:, 0], ids[:, 1]], axis=0).reshape(tokens, 128)

    gathered[my_block] = hidden_ref[...]

    place = lax.broadcasted_iota(jnp.int32, (1, tokens), 1) // rows
    teacher_id = jnp.zeros((1, tokens), F32)
    student_id = jnp.zeros((1, tokens), F32)
    for p in range(n):
        teacher_id = jnp.where(place == p, teacher_map[p].astype(F32), teacher_id)
        student_id = jnp.where(place == p, student_map[p].astype(F32), student_id)
    wanted = jnp.sum(jnp.where(eye, student_id, 0.0), axis=1, keepdims=True)
    same_row = (
        lax.broadcasted_iota(jnp.int32, (tokens, tokens), 0) % rows
        == lax.broadcasted_iota(jnp.int32, (tokens, tokens), 1) % rows
    )
    move = jnp.where(jnp.logical_and(wanted == teacher_id, same_row), 1.0, 0.0).astype(BF16)

    @pl.loop(0, n)
    def _(p):
        teacher_in(p).wait()

    for start, size in tiles(block, 256):
        piece = mine[:, :, start : start + size].astype(F32).reshape(tokens, size).astype(BF16)
        piece = jnp.dot(move, piece, preferred_element_type=F32)
        staged[:, :, start : start + size] = piece.reshape(n, rows, size).astype(BF16)

    pl.semaphore_wait(barrier, n - 1)

    def hidden_out(other):
        return remote(
            gathered.at[my_block], gathered.at[my_block], h_send.at[other], h_recv.at[chip], other * 2 + core
        )

    def hidden_in(other):
        return remote(
            gathered.at[core * chips + other], gathered.at[core * chips + other],
            h_send.at[other], h_recv.at[other], other * 2 + core,
        )

    def forward(other):
        return remote(
            gathered.at[core * chips + other], gathered.at[core * chips + other],
            f_send.at[other], f_recv.at[other], sibling,
        )

    def forwarded(other):
        return remote(
            gathered.at[(1 - core) * chips + other], gathered.at[(1 - core) * chips + other],
            f_send.at[other], f_recv.at[other], sibling,
        )

    @pl.loop(1, chips)
    def _(step):
        hidden_out((chip + step) % chips).start()

    forward(chip).start()

    def teacher_out(other):
        return remote(staged.at[other], teacher.at[me], t_send.at[other], t_recv.at[me], other)

    def teacher_from(other):
        return remote(staged.at[other], teacher.at[other], t_send.at[other], t_recv.at[other], other)

    @pl.loop(1, n)
    def _(step):
        teacher_out((me + step) % n).start()

    teacher[me] = staged[me]

    top = jnp.full((rows, 128), -jnp.inf, F32)
    top = lax.fori_loop(
        0, n,
        lambda j, top: functools.reduce(
            jnp.maximum,
            [staged[j, :, pl.ds(c, 128)].astype(F32) for c in range(0, block, 128)], top),
        top,
    )
    top = jnp.max(top, axis=1, keepdims=True)
    total = lax.fori_loop(
        0, n,
        lambda j, total: functools.reduce(
            jnp.add,
            [jnp.exp(staged[j, :, pl.ds(c, 128)].astype(F32) - top) for c in range(0, block, 128)], total),
        jnp.zeros((rows, 128), F32),
    )
    norm_mine = top + jnp.log(jnp.sum(total, axis=1, keepdims=True))

    @pl.loop(1, chips)
    def _(step):
        other = (chip + chips - step) % chips
        hidden_in(other).wait_recv()
        forward(other).start()

    def unpack(which):
        base = pl.multiple_of(which * half, half)
        flat = gathered[pl.ds(pl.multiple_of(which * chips, chips), chips)].astype(F32).reshape(half, width)
        hid[pl.ds(base, half), :] = flat.astype(BF16)
        hid_t[:, pl.ds(base, half)] = flat.T.astype(BF16)

    unpack(core)

    @pl.loop(0, chips)
    def _(other):
        forwarded(other).wait_recv()

    unpack(1 - core)
    head_in.wait()

    for start, size in tiles(block, 512):
        diff[:, start : start + size] = jnp.dot(
            hid[...], head[:, start : start + size], preferred_element_type=F32
        )

    lane = lax.broadcasted_iota(jnp.int32, (rows, 128), 1)

    @pl.loop(0, n)
    def _(b):
        at = pl.ds(pl.multiple_of(b * rows, rows), rows)
        logits = diff[at, :]
        peak = jnp.max(logits, axis=1, keepdims=True)
        e = jnp.exp(logits - peak)
        expo[at, :] = e
        mass = jnp.sum(e, axis=1, keepdims=True)
        stat[at, :] = jnp.where(lane == 0, peak, jnp.where(lane == 1, mass, 0.0))

    at = pl.ds(pl.multiple_of(my_block * rows, rows), rows)
    stat[at, :] = jnp.where(lane == 4, norm_mine, stat[at, :])

    column = lax.broadcasted_iota(jnp.int32, (rows, block), 1).astype(F32)

    @pl.loop(0, n)
    def _(step):
        other = (me + n - step) % n

        @pl.when(step > 0)
        def _():
            teacher_from(other).wait_recv()

        at = pl.ds(pl.multiple_of(slot(other) * rows, rows), rows)
        u = diff[at, :] - teacher[other].astype(F32)
        diff[at, :] = u
        cross = jnp.sum(expo[at, :] * u, axis=1, keepdims=True)
        hit = jnp.sum(jnp.where(column == tok_col[at, 0:1], u, 0.0), axis=1, keepdims=True)
        stat[at, :] = jnp.where(lane == 2, cross, jnp.where(lane == 3, hit, stat[at, :]))

    own = stat[...].T[0:8, :]
    stat_out[...] = own
    stat_in[me] = own

    def stat_to(other):
        return remote(stat_out, stat_in.at[me], s_send.at[other], s_recv.at[me], other)

    def stat_from(other):
        return remote(stat_out, stat_in.at[other], s_send.at[other], s_recv.at[other], other)

    @pl.loop(1, n)
    def _(step):
        stat_to((me + step) % n).start()

    @pl.loop(1, n)
    def _(step):
        stat_from((me + n - step) % n).wait_recv()

    peak = functools.reduce(jnp.maximum, [stat_in[d] for d in range(n)])[0:1, :]
    row = lax.broadcasted_iota(jnp.int32, (8, tokens), 0)
    weighted = jnp.logical_or(row == 1, row == 2)
    total = jnp.zeros((8, tokens), F32)
    for d in range(n):
        block_stat = stat_in[d]
        total = total + jnp.where(weighted, jnp.exp(block_stat[0:1, :] - peak), 1.0) * block_stat
    mass, cross, hit, norm_teacher = (total[i : i + 1, :] for i in range(1, 5))
    norm_student = peak + jnp.log(mass)
    mean = cross / mass
    sampled = hit - norm_student + norm_teacher
    div = mean - norm_student + norm_teacher
    scale = jnp.exp(own[0:1, :] - norm_student)
    shift = mean + sampled
    final = jnp.where(
        row == 0, scale, jnp.where(row == 1, shift, jnp.where(row == 2, sampled, jnp.where(row == 3, div, 0.0)))
    )
    columns = jnp.concatenate([final, jnp.zeros((120, tokens), F32)], axis=0).T
    stat[...] = columns
    halves = columns.reshape(2, chips, rows, 128)
    ordered = jnp.stack([halves[0], halves[1]], axis=1).reshape(tokens, 128)
    div_ref[...] = ordered.T[3:4, :]

    wide = lax.broadcasted_iota(jnp.int32, (2 * rows, block), 1).astype(F32)

    @pl.loop(0, n // 2)
    def _(b):
        at = pl.ds(pl.multiple_of(b * 2 * rows, 2 * rows), 2 * rows)
        g = expo[at, :] * (stat[at, 0:1] * (diff[at, :] - stat[at, 1:2]))
        g = g + jnp.where(wide == tok_col[at, 0:1], stat[at, 2:3], 0.0)
        grad[at, :] = g.astype(BF16)

    own_rows = pl.ds(pl.multiple_of(core * half, half), half)
    sib_rows = pl.ds(pl.multiple_of((1 - core) * half, half), half)
    pieces = tiles(width, 256)

    def pair(i):
        return remote(part_sib.at[i], pair_in.at[i], p_send.at[i], p_recv.at[i], sibling)

    for i, (start, size) in enumerate(pieces):
        part = lax.dot_general(
            grad[...], head[start : start + size, :], (((1,), (1,)), ((), ())), preferred_element_type=F32
        )
        stat_rows = jnp.where(core == 0, part[half:], part[:half])
        part_sib[i] = stat_rows
        part_own[i] = jnp.where(core == 0, part[:half], part[half:])
        pair(i).start()

    for i, (start, size) in enumerate(pieces):
        pair(i).wait_recv()
        total = part_own[i] + pair_in[i]
        part_own[i] = total
        red_out[:, :, start : start + size] = total.reshape(chips, rows, size).astype(BF16)

    def reduce_to(other):
        return remote(red_out.at[other], red_in.at[chip], r_send.at[other], r_recv.at[chip], other * 2 + core)

    def reduce_from(other):
        return remote(red_out.at[other], red_in.at[other], r_send.at[other], r_recv.at[other], other * 2 + core)

    @pl.loop(1, chips)
    def _(step):
        reduce_to((chip + step) % chips).start()

    red_in[chip] = jnp.zeros((rows, width), BF16)

    for start, size in tiles(block, 256):
        wgrad_ref[:, start : start + size] = jnp.dot(
            hid_t[...], grad[:, start : start + size], preferred_element_type=F32
        ).astype(BF16)

    @pl.loop(1, chips)
    def _(step):
        reduce_from((chip + chips - step) % chips).wait_recv()

    at = pl.ds(pl.multiple_of(chip * rows, rows), rows)
    for i, (start, size) in enumerate(pieces):
        total = part_own[i, at, :]
        for k in range(chips):
            total = total + red_in[k, :, start : start + size].astype(F32)
        hgrad_ref[:, start : start + size] = total.astype(BF16)

    @pl.loop(1, chips)
    def _(step):
        other = (chip + step) % chips
        hidden_out(other).wait_send()
        reduce_to(other).wait_send()

    @pl.loop(0, chips)
    def _(other):
        forward(other).wait_send()

    @pl.loop(1, n)
    def _(step):
        other = (me + step) % n
        teacher_out(other).wait_send()
        stat_to(other).wait_send()

    for i in range(len(pieces)):
        pair(i).wait_send()


def on_device(hidden, head_weight, teacher_logits, token_ids, teacher_map, student_map):
    n = lax.axis_size("voc")
    chips = n // 2
    rows, width = hidden.shape
    block = head_weight.shape[1]
    tokens = n * rows
    half = chips * rows
    pieces = len(tiles(width, 256))
    dma = pltpu.SemaphoreType.DMA
    vmem = pl.BlockSpec(memory_space=pltpu.VMEM)
    smem = pl.BlockSpec(memory_space=pltpu.SMEM)
    hbm = pl.BlockSpec(memory_space=pl.ANY)
    div, hgrad, wgrad = pl.pallas_call(
        functools.partial(kernel, n),
        out_shape=(
            jax.ShapeDtypeStruct((1, tokens), F32),
            jax.ShapeDtypeStruct((rows, width), BF16),
            pltpu.VMEM((width, block), BF16),
        ),
        in_specs=[vmem, hbm, hbm, vmem, smem, smem],
        out_specs=(vmem, vmem, vmem),
        scratch_shapes=[
            pltpu.VMEM((width, block), BF16),
            pltpu.VMEM((n, rows, block), BF16),
            pltpu.VMEM((n, rows, block), BF16),
            pltpu.VMEM((n, rows, block), BF16),
            pltpu.VMEM((n, rows, width), BF16),
            pltpu.VMEM((tokens, width), BF16),
            pltpu.VMEM((width, tokens), BF16),
            pltpu.VMEM((tokens, block), F32),
            pltpu.VMEM((tokens, block), F32),
            pltpu.VMEM((tokens, block), BF16),
            pltpu.VMEM((tokens, 128), F32),
            pltpu.VMEM((tokens, 128), F32),
            pltpu.VMEM((8, tokens), F32),
            pltpu.VMEM((n, 8, tokens), F32),
            pltpu.VMEM((pieces, half, 256), F32),
            pltpu.VMEM((pieces, half, 256), F32),
            pltpu.VMEM((pieces, half, 256), F32),
            pltpu.VMEM((chips, rows, width), BF16),
            pltpu.VMEM((chips, rows, width), BF16),
            dma((1,)),
            dma((n,)),
            dma((n,)),
            dma((n,)),
            dma((chips,)),
            dma((chips,)),
            dma((chips,)),
            dma((chips,)),
            dma((n,)),
            dma((n,)),
            dma((pieces,)),
            dma((pieces,)),
            dma((chips,)),
            dma((chips,)),
        ],
        compiler_params=pltpu.CompilerParams(
            collective_id=0, has_side_effects=True, vmem_limit_bytes=48 * 1024 * 1024
        ),
    )(hidden, head_weight, teacher_logits, token_ids.reshape(1, tokens), teacher_map, student_map)
    return div.reshape(tokens), hgrad, wgrad


def solution(mesh):
    return jax.shard_map(
        on_device,
        mesh=mesh,
        in_specs=(
            P(("grp", "voc"), None),
            P(None, "voc"),
            P(("grp", "voc"), None),
            P("grp"),
            P(),
            P(),
        ),
        out_specs=(P("grp"), P(("grp", "voc"), None), P(None, ("grp", "voc"))),
        check_vma=False,
    )
```

time: 411 us -> 65.3 us (0.16); the launches traced: 406 us -> 65.2 us
  blocking collectives: 356 us -> 0 us
  Pallas kernels: 0 us -> 60.7 us
  matrix products: 16.3 us -> 0 us
  other arithmetic: 11.2 us -> 0 us
  starting transfers between devices: 8.59 us -> 0 us
  local copies, waits for them, and re-layouts: 11.9 us -> 3.86 us
    psum x3 -> x0, blocking collectives: 260 us -> none  [the longest x1 132 us: on_device(): lax.psum(lax.dot_general(logit_grad, head_weight, (((1,), (1,)), ((), ())...]
    pmax x1 -> x0, blocking collectives: 62.2 us -> none  [on_device(): lax.pmax((jnp.max(logits, axis=1), jnp.max(teacher, axis=1)), 'voc')]
    pallas_call x0 -> x1, Pallas kernels: none -> 60.7 us  [on_device(): pl.pallas_call(functools.partial(kernel, n), out_shape=(jax.ShapeDtypeStr...]
    all_gather x1 -> x0, blocking collectives: 33.9 us -> none  [on_device(): all_hidden = lax.all_gather(hidden, 'voc', axis=0, tiled=True)]
    dot_general x3 -> x0, matrix products: 16.3 us -> none  [the longest x1 6.08 us: on_device(): jnp.dot(all_hidden, head_weight, preferred_element_type=jnp.float32)]
    all_to_all x1 -> x0, starting transfers between devices: 8.59 us -> none  [on_device(): lax.all_to_all(ordered, 'voc', split_axis=1, concat_axis=0, tiled=True)]
    reduce_sum x4 -> x0, other arithmetic: 6.43 us -> none  [the longest x1 2.83 us: on_device(): jnp.sum(jnp.where(sampled_mask, gap, 0.0), axis=1)]
    unnamed x11 -> x7, local copies, waits for them, and re-layouts: 9.76 us -> 3.86 us
  transfers between devices with their start and end apart: 1 -> 0, of which waited for: 0 -> 0; matrix products, arithmetic and copies ran while one was open for 2% -> 0% of each run, Pallas kernels for 0% -> 0%
where the time goes in v1:
time: 65.3 us; the launch traced here: 65.2 us
  Pallas kernels  60.7 us (93%)
  local copies, waits for them, and re-layouts  3.86 us (6%)
  between operations  0.66 us (1%)
    pallas_call x1, Pallas kernels, on_device(): pl.pallas_call(functools.partial(kernel, n), out_shape=(jax.ShapeDtypeStr...  60.7 us
    unnamed x7, local copies, waits for them, and re-layouts  3.86 us

profile of v1, /device:TPU:1, one launch (start us, length us, event | category | flops | bytes accessed | tf_op | source)
XLA Modules:
  0.0 65.2 jit_solution(17389219265093772699)
XLA Ops:
  0.6 60.7 %shard_map.85 = (f32[1,256]{1,0:T(1,128)}, bf16[8,1280]{1,0:T(8,128)(2,1)}, bf16[1280,2432]{1,0:T(8,128)(2,1)S(1)}) custom-call(bf16[8,1280]{1,0:T(8,128)(2,1)} %hidden_ref.1, bf16[1280,2432]{1,0:T(8,128)(2,1)} %head_ref.1, bf16[8,77824]{1,0:T(8,128)(2,1)} %teacher_ref.1, s32[1,256]{1,0:T(1,128)} %bitcast.3, s32[32]{0:T(128)} %teacher_map.1, s32[32]{0:T(128)} %student_map.1), custom_call_target="tpu_custom_call" | custom-call | tf_op jit(solution)/shard_map/pallas_call | solution.py:385
  61.3 0.0 copy-start.1
  61.3 0.0 copy-start
  61.3 2.7 %copy.12 = bf16[1280,2432]{1,0:T(8,128)(2,1)} copy(bf16[1280,2432]{1,0:T(8,128)(2,1)S(1)} %get-tuple-element.11) | data formatting | bytes 12451840
  64.0 0.0 copy-done.1
  64.0 0.6 copy.13
  64.6 0.0 copy-done
  64.6 0.6 copy.14
Async XLA Ops:
  61.3 2.7 %copy-start.1 = (f32[1,256]{1,0:T(1,128)S(1)}, f32[1,256]{1,0:T(1,128)}, u32[]{:S(2)}) copy-start(f32[1,256]{1,0:T(1,128)} %get-tuple-element.6) | copy-start | bytes 3076
  61.3 3.3 %copy-start = (bf16[8,1280]{1,0:T(8,128)(2,1)S(1)}, bf16[8,1280]{1,0:T(8,128)(2,1)}, u32[]{:S(2)}) copy-start(bf16[8,1280]{1,0:T(8,128)(2,1)} %get-tuple-element.16) | copy-start | bytes 61444

commit v2 on v1

--- a/solution.py
+++ b/solution.py
@@ -21,12 +21,15 @@
     hidden_ref,
     head_ref,
     teacher_ref,
+    token_hbm,
+    teacher_map_hbm,
+    student_map_hbm,
+    div_ref,
+    hgrad_ref,
+    wgrad_ref,
     token_ref,
     teacher_map,
     student_map,
-    div_ref,
-    hgrad_ref,
-    wgrad_ref,
     head,
     mine,
     staged,
@@ -34,11 +37,16 @@
     gathered,
     hid,
     hid_t,
+    grad,
     diff,
     expo,
-    grad,
     tok_col,
     stat,
+    peaks,
+    masses,
+    norms,
+    crosses,
+    hits,
     stat_out,
     stat_in,
     part_sib,
@@ -86,6 +94,15 @@
     def _(step):
         pl.semaphore_signal(barrier, inc=1, device_id={"voc": (me + step) % n}, device_id_type=MESH)
 
+    small = [
+        pltpu.make_async_copy(token_hbm, token_ref, local_sem.at[1]),
+        pltpu.make_async_copy(teacher_map_hbm, teacher_map, local_sem.at[2]),
+        pltpu.make_async_copy(student_map_hbm, student_map, local_sem.at[3]),
+        pltpu.make_async_copy(hidden_ref, gathered.at[my_block], local_sem.at[4]),
+    ]
+    for copy in small:
+        copy.start()
+
     def teacher_in(p):
         return pltpu.make_async_copy(
             teacher_ref.at[:, pl.ds(pl.multiple_of(p * block, 128), block)], mine.at[p], m_sem.at[p]
@@ -97,6 +114,9 @@
 
     head_in = pltpu.make_async_copy(head_ref, head, local_sem.at[0])
     head_in.start()
+
+    for copy in small:
+        copy.wait()
 
     eye = (
         lax.broadcasted_iota(jnp.int32, (tokens, tokens), 0)
@@ -106,8 +126,6 @@
     ids = ids - (student_map[me] * block).astype(F32)
     ids = jnp.broadcast_to(ids, (tokens, 128)).reshape(chips, 2, rows, 128)
     tok_col[...] = jnp.concatenate([ids[:, 0], ids[:, 1]], axis=0).reshape(tokens, 128)
-
-    gathered[my_block] = hidden_ref[...]
 
     place = lax.broadcasted_iota(jnp.int32, (1, tokens), 1) // rows
     teacher_id = jnp.zeros((1, tokens), F32)
@@ -174,23 +192,31 @@
 
     teacher[me] = staged[me]
 
-    top = jnp.full((rows, 128), -jnp.inf, F32)
+    spots = [c for c, _ in tiles(block, 128)]
+
+    def spread(op, values, carry):
+        carry = list(carry)
+        for i, value in enumerate(values):
+            carry[i % 4] = op(carry[i % 4], value)
+        return tuple(carry)
+
+    def gather4(op, carry):
+        return op(op(carry[0], carry[1]), op(carry[2], carry[3]))
+
     top = lax.fori_loop(
         0, n,
-        lambda j, top: functools.reduce(
-            jnp.maximum,
-            [staged[j, :, pl.ds(c, 128)].astype(F32) for c in range(0, block, 128)], top),
-        top,
+        lambda j, carry: spread(jnp.maximum, [staged[j, :, c : c + 128].astype(F32) for c in spots], carry),
+        (jnp.full((rows, 128), -jnp.inf, F32),) * 4,
     )
-    top = jnp.max(top, axis=1, keepdims=True)
+    top = jnp.max(gather4(jnp.maximum, top), axis=1, keepdims=True)
     total = lax.fori_loop(
         0, n,
-        lambda j, total: functools.reduce(
-            jnp.add,
-            [jnp.exp(staged[j, :, pl.ds(c, 128)].astype(F32) - top) for c in range(0, block, 128)], total),
-        jnp.zeros((rows, 128), F32),
+        lambda j, carry: spread(
+            jnp.add, [jnp.exp(staged[j, :, c : c + 128].astype(F32) - top) for c in spots], carry
+        ),
+        (jnp.zeros((rows, 128), F32),) * 4,
     )
-    norm_mine = top + jnp.log(jnp.sum(total, axis=1, keepdims=True))
+    norm_mine = top + jnp.log(jnp.sum(gather4(jnp.add, total), axis=1, keepdims=True))
 
     @pl.loop(1, chips)
     def _(step):
@@ -218,22 +244,31 @@
             hid[...], head[:, start : start + size], preferred_element_type=F32
         )
 
-    lane = lax.broadcasted_iota(jnp.int32, (rows, 128), 1)
-
-    @pl.loop(0, n)
+    group = 64
+
+    @pl.loop(0, tokens // group)
     def _(b):
-        at = pl.ds(pl.multiple_of(b * rows, rows), rows)
-        logits = diff[at, :]
-        peak = jnp.max(logits, axis=1, keepdims=True)
-        e = jnp.exp(logits - peak)
-        expo[at, :] = e
-        mass = jnp.sum(e, axis=1, keepdims=True)
-        stat[at, :] = jnp.where(lane == 0, peak, jnp.where(lane == 1, mass, 0.0))
-
-    at = pl.ds(pl.multiple_of(my_block * rows, rows), rows)
-    stat[at, :] = jnp.where(lane == 4, norm_mine, stat[at, :])
-
-    column = lax.broadcasted_iota(jnp.int32, (rows, block), 1).astype(F32)
+        at = pl.ds(pl.multiple_of(b * group, group), group)
+        top = diff[at, 0:128]
+        for c in spots[1:]:
+            top = jnp.maximum(top, diff[at, c : c + 128])
+        top = jnp.broadcast_to(jnp.max(top, axis=1, keepdims=True), (group, 128))
+        peaks[at, :] = top
+        total = jnp.zeros((group, 128), F32)
+        for c in spots:
+            e = jnp.exp(diff[at, c : c + 128] - top)
+            expo[at, c : c + 128] = e
+            total = total + e
+        masses[at, :] = total
+
+    norms[...] = jnp.zeros_like(norms)
+    norms[pl.ds(pl.multiple_of(my_block * rows, rows), rows), :] = jnp.broadcast_to(norm_mine, (rows, 128))
+    early = [
+        peaks[...].T[0:1, :],
+        jnp.sum(masses[...].T, axis=0, keepdims=True),
+        norms[...].T[0:1, :],
+    ]
+    lane = lax.broadcasted_iota(jnp.int32, (rows, 128), 1).astype(F32)
 
     @pl.loop(0, n)
     def _(step):
@@ -244,13 +279,31 @@
             teacher_from(other).wait_recv()
 
         at = pl.ds(pl.multiple_of(slot(other) * rows, rows), rows)
-        u = diff[at, :] - teacher[other].astype(F32)
-        diff[at, :] = u
-        cross = jnp.sum(expo[at, :] * u, axis=1, keepdims=True)
-        hit = jnp.sum(jnp.where(column == tok_col[at, 0:1], u, 0.0), axis=1, keepdims=True)
-        stat[at, :] = jnp.where(lane == 2, cross, jnp.where(lane == 3, hit, stat[at, :]))
-
-    own = stat[...].T[0:8, :]
+        picked = tok_col[at, :] - lane
+        cross = [jnp.zeros((rows, 128), F32)] * 4
+        hit = [jnp.zeros((rows, 128), F32)] * 4
+        for i, c in enumerate(spots):
+            u = diff[at, c : c + 128] - teacher[other, :, c : c + 128].astype(F32)
+            diff[at, c : c + 128] = u
+            cross[i % 4] = cross[i % 4] + expo[at, c : c + 128] * u
+            hit[i % 4] = hit[i % 4] + jnp.where(picked == float(c), u, 0.0)
+        crosses[at, :] = gather4(jnp.add, cross)
+        hits[at, :] = gather4(jnp.add, hit)
+
+    row = lax.broadcasted_iota(jnp.int32, (8, tokens), 0)
+
+    def rows_of(values):
+        out = jnp.zeros((8, tokens), F32)
+        for i, value in enumerate(values):
+            out = jnp.where(row == i, value, out)
+        return out
+
+    own = rows_of([
+        early[0], early[1],
+        jnp.sum(crosses[...].T, axis=0, keepdims=True),
+        jnp.sum(hits[...].T, axis=0, keepdims=True),
+        early[2],
+    ])
     stat_out[...] = own
     stat_in[me] = own
 
@@ -269,7 +322,6 @@
         stat_from((me + n - step) % n).wait_recv()
 
     peak = functools.reduce(jnp.maximum, [stat_in[d] for d in range(n)])[0:1, :]
-    row = lax.broadcasted_iota(jnp.int32, (8, tokens), 0)
     weighted = jnp.logical_or(row == 1, row == 2)
     total = jnp.zeros((8, tokens), F32)
     for d in range(n):
@@ -282,23 +334,27 @@
     div = mean - norm_student + norm_teacher
     scale = jnp.exp(own[0:1, :] - norm_student)
     shift = mean + sampled
-    final = jnp.where(
-        row == 0, scale, jnp.where(row == 1, shift, jnp.where(row == 2, sampled, jnp.where(row == 3, div, 0.0)))
-    )
+    final = rows_of([scale, shift, sampled, div])
     columns = jnp.concatenate([final, jnp.zeros((120, tokens), F32)], axis=0).T
     stat[...] = columns
     halves = columns.reshape(2, chips, rows, 128)
     ordered = jnp.stack([halves[0], halves[1]], axis=1).reshape(tokens, 128)
     div_ref[...] = ordered.T[3:4, :]
 
-    wide = lax.broadcasted_iota(jnp.int32, (2 * rows, block), 1).astype(F32)
-
-    @pl.loop(0, n // 2)
+    span = 32
+
+    @pl.loop(0, tokens // span)
     def _(b):
-        at = pl.ds(pl.multiple_of(b * 2 * rows, 2 * rows), 2 * rows)
-        g = expo[at, :] * (stat[at, 0:1] * (diff[at, :] - stat[at, 1:2]))
-        g = g + jnp.where(wide == tok_col[at, 0:1], stat[at, 2:3], 0.0)
-        grad[at, :] = g.astype(BF16)
+        at = pl.ds(pl.multiple_of(b * span, span), span)
+        wide = lax.broadcasted_iota(jnp.int32, (span, 128), 1).astype(F32)
+        picked = tok_col[at, :] - wide
+        scale = jnp.broadcast_to(stat[at, 0:1], (span, 128))
+        shift = jnp.broadcast_to(stat[at, 1:2], (span, 128))
+        sampled = jnp.broadcast_to(stat[at, 2:3], (span, 128))
+        for c in spots:
+            g = expo[at, c : c + 128] * (scale * (diff[at, c : c + 128] - shift))
+            g = g + jnp.where(picked == float(c), sampled, 0.0)
+            grad[at, c : c + 128] = g.astype(BF16)
 
     own_rows = pl.ds(pl.multiple_of(core * half, half), half)
     sib_rows = pl.ds(pl.multiple_of((1 - core) * half, half), half)
@@ -368,6 +424,20 @@
 
     for i in range(len(pieces)):
         pair(i).wait_send()
+
+
+def out_kernel(div, hgrad, wgrad, div_out, hgrad_out, wgrad_out, sem):
+    strip = wgrad.shape[0] // 8
+    copies = [
+        pltpu.make_async_copy(wgrad.at[pl.ds(i * strip, strip)], wgrad_out.at[pl.ds(i * strip, strip)], sem.at[i])
+        for i in range(8)
+    ]
+    copies.append(pltpu.make_async_copy(div, div_out, sem.at[8]))
+    copies.append(pltpu.make_async_copy(hgrad, hgrad_out, sem.at[9]))
+    for copy in copies:
+        copy.start()
+    for copy in copies:
+        copy.wait()
 
 
 def on_device(hidden, head_weight, teacher_logits, token_ids, teacher_map, student_map):
@@ -380,18 +450,20 @@
     pieces = len(tiles(width, 256))
     dma = pltpu.SemaphoreType.DMA
     vmem = pl.BlockSpec(memory_space=pltpu.VMEM)
-    smem = pl.BlockSpec(memory_space=pltpu.SMEM)
-    hbm = pl.BlockSpec(memory_space=pl.ANY)
+    hbm = pl.BlockSpec(memory_space=pltpu.HBM)
     div, hgrad, wgrad = pl.pallas_call(
         functools.partial(kernel, n),
         out_shape=(
-            jax.ShapeDtypeStruct((1, tokens), F32),
-            jax.ShapeDtypeStruct((rows, width), BF16),
+            pltpu.VMEM((1, tokens), F32),
+            pltpu.VMEM((rows, width), BF16),
             pltpu.VMEM((width, block), BF16),
         ),
-        in_specs=[vmem, hbm, hbm, vmem, smem, smem],
+        in_specs=[hbm] * 6,
         out_specs=(vmem, vmem, vmem),
         scratch_shapes=[
+            pltpu.VMEM((1, tokens), jnp.int32),
+            pltpu.SMEM((n,), jnp.int32),
+            pltpu.SMEM((n,), jnp.int32),
             pltpu.VMEM((width, block), BF16),
             pltpu.VMEM((n, rows, block), BF16),
             pltpu.VMEM((n, rows, block), BF16),
@@ -399,9 +471,14 @@
             pltpu.VMEM((n, rows, width), BF16),
             pltpu.VMEM((tokens, width), BF16),
             pltpu.VMEM((width, tokens), BF16),
+            pltpu.VMEM((tokens, block), BF16),
             pltpu.VMEM((tokens, block), F32),
             pltpu.VMEM((tokens, block), F32),
-            pltpu.VMEM((tokens, block), BF16),
+            pltpu.VMEM((tokens, 128), F32),
+            pltpu.VMEM((tokens, 128), F32),
+            pltpu.VMEM((tokens, 128), F32),
+            pltpu.VMEM((tokens, 128), F32),
+            pltpu.VMEM((tokens, 128), F32),
             pltpu.VMEM((tokens, 128), F32),
             pltpu.VMEM((tokens, 128), F32),
             pltpu.VMEM((8, tokens), F32),
@@ -411,7 +488,7 @@
             pltpu.VMEM((pieces, half, 256), F32),
             pltpu.VMEM((chips, rows, width), BF16),
             pltpu.VMEM((chips, rows, width), BF16),
-            dma((1,)),
+            dma((5,)),
             dma((n,)),
             dma((n,)),
             dma((n,)),
@@ -429,7 +506,22 @@
         compiler_params=pltpu.CompilerParams(
             collective_id=0, has_side_effects=True, vmem_limit_bytes=48 * 1024 * 1024
         ),
-    )(hidden, head_weight, teacher_logits, token_ids.reshape(1, tokens), teacher_map, student_map)
+    )(*(
+        pltpu.with_memory_space_constraint(x, pltpu.HBM)
+        for x in (hidden, head_weight, teacher_logits, token_ids.reshape(1, tokens), teacher_map, student_map)
+    ))
+    div, hgrad, wgrad = pl.pallas_call(
+        out_kernel,
+        out_shape=(
+            jax.ShapeDtypeStruct((1, tokens), F32),
+            jax.ShapeDtypeStruct((rows, width), BF16),
+            jax.ShapeDtypeStruct((width, block), BF16),
+        ),
+        in_specs=[vmem] * 3,
+        out_specs=(hbm,) * 3,
+        scratch_shapes=[dma((10,))],
+        compiler_params=pltpu.CompilerParams(vmem_limit_bytes=2 * 1024 * 1024),
+    )(*(pltpu.with_memory_space_constraint(x, pltpu.VMEM) for x in (div, hgrad, wgrad)))
     return div.reshape(tokens), hgrad, wgrad
 
 

time: 65.3 us -> 54.7 us (0.84)
  Pallas kernels: 60.7 us -> 54 us
  local copies, waits for them, and re-layouts: 3.86 us -> 0 us
    pallas_call x1 -> x2, Pallas kernels: 60.7 us -> 54 us  [the longest x1 51.2 us: on_device(): pl.pallas_call(functools.partial(kernel, n), out_shape=(pltpu.VMEM((1, to...]
    unnamed x7 -> x0, local copies, waits for them, and re-layouts: 3.86 us -> none
where the time goes in v2:
time: 54.7 us; the launch traced here: 54.6 us
  Pallas kernels  54 us (99%)
  between operations  0.64 us (1%)
    pallas_call x1, Pallas kernels, on_device(): pl.pallas_call(functools.partial(kernel, n), out_shape=(pltpu.VMEM((1, to...  51.2 us
    pallas_call x1, Pallas kernels, on_device(): pl.pallas_call(out_kernel, out_shape=(jax.ShapeDtypeStruct((1, tokens), F...  2.74 us

profile of v2, /device:TPU:1, one launch (start us, length us, event | category | flops | bytes accessed | tf_op | source)
XLA Modules:
  0.0 54.6 jit_solution(3105354233504319918)
XLA Ops:
  0.6 51.2 %shard_map.85 = (f32[1,256]{1,0:T(1,128)S(1)}, bf16[8,1280]{1,0:T(8,128)(2,1)S(1)}, bf16[1280,2432]{1,0:T(8,128)(2,1)S(1)}) custom-call(bf16[8,1280]{1,0:T(8,128)(2,1)} %hidden_ref.1, bf16[1280,2432]{1,0:T(8,128)(2,1)} %head_ref.1, bf16[8,77824]{1,0:T(8,128)(2,1)} %teacher_ref.1, s32[1,256]{1,0:T(1,128)} %bitcast.2, s32[32]{0:T(128)} %teacher_map_hbm.1, ...), custom_call_target="tpu_custom_call" | custom-call | tf_op jit(solution)/shard_map/pallas_call | solution.py:454
  51.9 2.7 %shard_map.86 = (f32[1,256]{1,0:T(1,128)}, bf16[8,1280]{1,0:T(8,128)(2,1)}, bf16[1280,2432]{1,0:T(8,128)(2,1)}) custom-call(f32[1,256]{1,0:T(1,128)S(1)} %get-tuple-element.9.div, bf16[8,1280]{1,0:T(8,128)(2,1)S(1)} %get-tuple-element.10.hgrad, bf16[1280,2432]{1,0:T(8,128)(2,1)S(1)} %get-tuple-element.11.wgrad), custom_call_target="tpu_custom_call" | custom-call | tf_op jit(solution)/shard_map/pallas_call | solution.py:513

commit v3 on v2

--- a/solution.py
+++ b/solution.py
@@ -1,4 +1,5 @@
 import functools
+import math
 
 import jax
 import jax.numpy as jnp
@@ -74,13 +75,36 @@
     block = head_ref.shape[1]
     half = chips * rows
     tokens = 2 * half
+    side = math.isqrt(chips)
     me = lax.axis_index("voc")
-    core, chip = me % 2, me // 2
+    core, chip = lax.rem(me, 2), lax.div(me, 2)
+    y, x = lax.div(chip, side), lax.rem(chip, side)
     sibling = me + 1 - 2 * core
     my_block = core * chips + chip
 
-    def slot(device):
-        return (device % 2) * chips + device // 2
+    ys = [lax.rem(y + d, side) * side for d in range(side)]
+    xs = [lax.rem(x + d, side) for d in range(side)]
+
+    def far(d):
+        return -sum(min(v, side - v) for v in d[:2])
+
+    def back(d):
+        return (-d[0] % side, -d[1] % side) + d[2:]
+
+    chip_deltas = sorted([(dy, dx) for dy in range(side) for dx in range(side) if dy or dx], key=far)
+    device_deltas = sorted([d + (c,) for d in chip_deltas + [(0, 0)] for c in (0, 1)][:-2], key=far) + [(0, 0, 1)]
+    cores = [core, 1 - core]
+
+    def chip_at(d):
+        return ys[d[0]] + xs[d[1]]
+
+    def device_at(d):
+        return chip_at(d) * 2 + cores[d[2]]
+
+    chip_to = [chip_at(d) for d in chip_deltas]
+    chip_from = [chip_at(back(d)) for d in chip_deltas]
+    device_to = [device_at(d) for d in device_deltas]
+    device_from = [device_at(back(d)) for d in device_deltas]
 
     def remote(src, dst, send, recv, device):
         return pltpu.make_async_remote_copy(
@@ -90,9 +114,8 @@
 
     barrier = pltpu.get_barrier_semaphore()
 
-    @pl.loop(1, n)
-    def _(step):
-        pl.semaphore_signal(barrier, inc=1, device_id={"voc": (me + step) % n}, device_id_type=MESH)
+    for other in device_to:
+        pl.semaphore_signal(barrier, inc=1, device_id={"voc": other}, device_id_type=MESH)
 
     small = [
         pltpu.make_async_copy(token_hbm, token_ref, local_sem.at[1]),
@@ -151,44 +174,36 @@
 
     pl.semaphore_wait(barrier, n - 1)
 
-    def hidden_out(other):
+    def hidden_out(i):
         return remote(
-            gathered.at[my_block], gathered.at[my_block], h_send.at[other], h_recv.at[chip], other * 2 + core
+            gathered.at[my_block], gathered.at[my_block], h_send.at[i], h_recv.at[i], chip_to[i] * 2 + core
         )
 
-    def hidden_in(other):
-        return remote(
-            gathered.at[core * chips + other], gathered.at[core * chips + other],
-            h_send.at[other], h_recv.at[other], other * 2 + core,
-        )
-
-    def forward(other):
-        return remote(
-            gathered.at[core * chips + other], gathered.at[core * chips + other],
-            f_send.at[other], f_recv.at[other], sibling,
-        )
-
-    def forwarded(other):
-        return remote(
-            gathered.at[(1 - core) * chips + other], gathered.at[(1 - core) * chips + other],
-            f_send.at[other], f_recv.at[other], sibling,
-        )
-
-    @pl.loop(1, chips)
-    def _(step):
-        hidden_out((chip + step) % chips).start()
-
-    forward(chip).start()
-
-    def teacher_out(other):
-        return remote(staged.at[other], teacher.at[me], t_send.at[other], t_recv.at[me], other)
+    def hidden_in(i):
+        landed = gathered.at[core * chips + chip_from[i]]
+        return remote(landed, landed, h_send.at[i], h_recv.at[i], chip_to[i] * 2 + core)
+
+    def forward(i):
+        landed = gathered.at[my_block if i == chips - 1 else core * chips + chip_from[i]]
+        return remote(landed, landed, f_send.at[i], f_recv.at[i], sibling)
+
+    def forwarded(i):
+        landed = gathered.at[(1 - core) * chips + (chip if i == chips - 1 else chip_from[i])]
+        return remote(landed, landed, f_send.at[i], f_recv.at[i], sibling)
+
+    for i in range(chips - 1):
+        hidden_out(i).start()
+    forward(chips - 1).start()
+
+    def teacher_out(i):
+        other = device_to[i]
+        return remote(staged.at[other], teacher.at[me], t_send.at[i], t_recv.at[me], other)
 
     def teacher_from(other):
-        return remote(staged.at[other], teacher.at[other], t_send.at[other], t_recv.at[other], other)
-
-    @pl.loop(1, n)
-    def _(step):
-        teacher_out((me + step) % n).start()
+        return remote(staged.at[other], teacher.at[other], t_send.at[0], t_recv.at[other], other)
+
+    for i in range(n - 1):
+        teacher_out(i).start()
 
     teacher[me] = staged[me]
 
@@ -218,11 +233,9 @@
     )
     norm_mine = top + jnp.log(jnp.sum(gather4(jnp.add, total), axis=1, keepdims=True))
 
-    @pl.loop(1, chips)
-    def _(step):
-        other = (chip + chips - step) % chips
-        hidden_in(other).wait_recv()
-        forward(other).start()
+    for i in range(chips - 1):
+        hidden_in(i).wait_recv()
+        forward(i).start()
 
     def unpack(which):
         base = pl.multiple_of(which * half, half)
@@ -232,9 +245,8 @@
 
     unpack(core)
 
-    @pl.loop(0, chips)
-    def _(other):
-        forwarded(other).wait_recv()
+    for i in range(chips):
+        forwarded(i).wait_recv()
 
     unpack(1 - core)
     head_in.wait()
@@ -263,22 +275,23 @@
 
     norms[...] = jnp.zeros_like(norms)
     norms[pl.ds(pl.multiple_of(my_block * rows, rows), rows), :] = jnp.broadcast_to(norm_mine, (rows, 128))
-    early = [
-        peaks[...].T[0:1, :],
-        jnp.sum(masses[...].T, axis=0, keepdims=True),
-        norms[...].T[0:1, :],
-    ]
+    peak = peaks[...].T[0:1, :]
+    mass = jnp.sum(masses[...].T, axis=0, keepdims=True)
+    lse = peak + jnp.log(mass)
+    norm_row = norms[...].T[0:1, :]
     lane = lax.broadcasted_iota(jnp.int32, (rows, 128), 1).astype(F32)
 
     @pl.loop(0, n)
     def _(step):
-        other = (me + n - step) % n
-
-        @pl.when(step > 0)
+        near_y = lax.rem(y + 2 + lax.div(step, 2 * side), side)
+        near_x = lax.rem(x + 2 + lax.div(step, 2), side)
+        other = (near_y * side + near_x) * 2 + lax.rem(step, 2)
+
+        @pl.when(other != me)
         def _():
             teacher_from(other).wait_recv()
 
-        at = pl.ds(pl.multiple_of(slot(other) * rows, rows), rows)
+        at = pl.ds(pl.multiple_of((lax.rem(step, 2) * chips + near_y * side + near_x) * rows, rows), rows)
         picked = tok_col[at, :] - lane
         cross = [jnp.zeros((rows, 128), F32)] * 4
         hit = [jnp.zeros((rows, 128), F32)] * 4
@@ -290,52 +303,49 @@
         crosses[at, :] = gather4(jnp.add, cross)
         hits[at, :] = gather4(jnp.add, hit)
 
-    row = lax.broadcasted_iota(jnp.int32, (8, tokens), 0)
+    row = lax.broadcasted_iota(jnp.int32, (4, tokens), 0)
 
     def rows_of(values):
-        out = jnp.zeros((8, tokens), F32)
+        out = jnp.zeros((4, tokens), F32)
         for i, value in enumerate(values):
             out = jnp.where(row == i, value, out)
         return out
 
     own = rows_of([
-        early[0], early[1],
-        jnp.sum(crosses[...].T, axis=0, keepdims=True),
+        lse,
+        jnp.sum(crosses[...].T, axis=0, keepdims=True) / mass,
         jnp.sum(hits[...].T, axis=0, keepdims=True),
-        early[2],
+        norm_row,
     ])
     stat_out[...] = own
     stat_in[me] = own
 
-    def stat_to(other):
-        return remote(stat_out, stat_in.at[me], s_send.at[other], s_recv.at[me], other)
-
-    def stat_from(other):
-        return remote(stat_out, stat_in.at[other], s_send.at[other], s_recv.at[other], other)
-
-    @pl.loop(1, n)
-    def _(step):
-        stat_to((me + step) % n).start()
-
-    @pl.loop(1, n)
-    def _(step):
-        stat_from((me + n - step) % n).wait_recv()
-
-    peak = functools.reduce(jnp.maximum, [stat_in[d] for d in range(n)])[0:1, :]
-    weighted = jnp.logical_or(row == 1, row == 2)
-    total = jnp.zeros((8, tokens), F32)
+    def stat_to(i):
+        return remote(stat_out, stat_in.at[me], s_send.at[i], s_recv.at[i], device_to[i])
+
+    def stat_from(i):
+        return remote(stat_out, stat_in.at[device_from[i]], s_send.at[i], s_recv.at[i], device_to[i])
+
+    for i in range(n - 1):
+        stat_to(i).start()
+    for i in range(n - 1):
+        stat_from(i).wait_recv()
+
+    top = functools.reduce(jnp.maximum, [stat_in[d] for d in range(n)])[0:1, :]
+    total = jnp.zeros((4, tokens), F32)
     for d in range(n):
         block_stat = stat_in[d]
-        total = total + jnp.where(weighted, jnp.exp(block_stat[0:1, :] - peak), 1.0) * block_stat
-    mass, cross, hit, norm_teacher = (total[i : i + 1, :] for i in range(1, 5))
-    norm_student = peak + jnp.log(mass)
+        weight = jnp.exp(block_stat[0:1, :] - top)
+        total = total + jnp.where(row == 0, weight, jnp.where(row == 1, weight * block_stat, block_stat))
+    mass, cross, hit, norm_teacher = (total[i : i + 1, :] for i in range(4))
+    norm_student = top + jnp.log(mass)
     mean = cross / mass
     sampled = hit - norm_student + norm_teacher
     div = mean - norm_student + norm_teacher
-    scale = jnp.exp(own[0:1, :] - norm_student)
+    scale = jnp.exp(peak - norm_student)
     shift = mean + sampled
     final = rows_of([scale, shift, sampled, div])
-    columns = jnp.concatenate([final, jnp.zeros((120, tokens), F32)], axis=0).T
+    columns = jnp.concatenate([final, jnp.zeros((124, tokens), F32)], axis=0).T
     stat[...] = columns
     halves = columns.reshape(2, chips, rows, 128)
     ordered = jnp.stack([halves[0], halves[1]], axis=1).reshape(tokens, 128)
@@ -378,15 +388,14 @@
         part_own[i] = total
         red_out[:, :, start : start + size] = total.reshape(chips, rows, size).astype(BF16)
 
-    def reduce_to(other):
-        return remote(red_out.at[other], red_in.at[chip], r_send.at[other], r_recv.at[chip], other * 2 + core)
-
-    def reduce_from(other):
-        return remote(red_out.at[other], red_in.at[other], r_send.at[other], r_recv.at[other], other * 2 + core)
-
-    @pl.loop(1, chips)
-    def _(step):
-        reduce_to((chip + step) % chips).start()
+    def reduce_to(i):
+        return remote(red_out.at[chip_to[i]], red_in.at[chip], r_send.at[i], r_recv.at[i], chip_to[i] * 2 + core)
+
+    def reduce_from(i):
+        return remote(red_out.at[chip], red_in.at[chip_from[i]], r_send.at[i], r_recv.at[i], chip_to[i] * 2 + core)
+
+    for i in range(chips - 1):
+        reduce_to(i).start()
 
     red_in[chip] = jnp.zeros((rows, width), BF16)
 
@@ -395,9 +404,8 @@
             hid_t[...], grad[:, start : start + size], preferred_element_type=F32
         ).astype(BF16)
 
-    @pl.loop(1, chips)
-    def _(step):
-        reduce_from((chip + chips - step) % chips).wait_recv()
+    for i in range(chips - 1):
+        reduce_from(i).wait_recv()
 
     at = pl.ds(pl.multiple_of(chip * rows, rows), rows)
     for i, (start, size) in enumerate(pieces):
@@ -406,22 +414,14 @@
             total = total + red_in[k, :, start : start + size].astype(F32)
         hgrad_ref[:, start : start + size] = total.astype(BF16)
 
-    @pl.loop(1, chips)
-    def _(step):
-        other = (chip + step) % chips
-        hidden_out(other).wait_send()
-        reduce_to(other).wait_send()
-
-    @pl.loop(0, chips)
-    def _(other):
-        forward(other).wait_send()
-
-    @pl.loop(1, n)
-    def _(step):
-        other = (me + step) % n
-        teacher_out(other).wait_send()
-        stat_to(other).wait_send()
-
+    for i in range(chips - 1):
+        hidden_out(i).wait_send()
+        reduce_to(i).wait_send()
+    for i in range(chips):
+        forward(i).wait_send()
+    for i in range(n - 1):
+        teacher_out(i).wait_send()
+        stat_to(i).wait_send()
     for i in range(len(pieces)):
         pair(i).wait_send()
 
@@ -481,8 +481,8 @@
             pltpu.VMEM((tokens, 128), F32),
             pltpu.VMEM((tokens, 128), F32),
             pltpu.VMEM((tokens, 128), F32),
-            pltpu.VMEM((8, tokens), F32),
-            pltpu.VMEM((n, 8, tokens), F32),
+            pltpu.VMEM((4, tokens), F32),
+            pltpu.VMEM((n, 4, tokens), F32),
             pltpu.VMEM((pieces, half, 256), F32),
             pltpu.VMEM((pieces, half, 256), F32),
             pltpu.VMEM((pieces, half, 256), F32),

time: 54.7 us -> 52.6 us (0.962)
  Pallas kernels: 54 us -> 51.8 us
    pallas_call x1, Pallas kernels: 51.2 us -> 49.1 us  [on_device(): pl.pallas_call(functools.partial(kernel, n), out_shape=(pltpu.VMEM((1, to...]
where the time goes in v3:
time: 52.6 us; the launch traced here: 52.5 us
  Pallas kernels  51.8 us (98%)
  between operations  0.64 us (1%)
    pallas_call x1, Pallas kernels, on_device(): pl.pallas_call(functools.partial(kernel, n), out_shape=(pltpu.VMEM((1, to...  49.1 us
    pallas_call x1, Pallas kernels, on_device(): pl.pallas_call(out_kernel, out_shape=(jax.ShapeDtypeStruct((1, tokens), F...  2.74 us

profile of v3, /device:TPU:1, one launch (start us, length us, event | category | flops | bytes accessed | tf_op | source)
XLA Modules:
  0.0 52.5 jit_solution(5959206850223279110)
XLA Ops:
  0.6 49.1 %shard_map.85 = (f32[1,256]{1,0:T(1,128)S(1)}, bf16[8,1280]{1,0:T(8,128)(2,1)S(1)}, bf16[1280,2432]{1,0:T(8,128)(2,1)S(1)}) custom-call(bf16[8,1280]{1,0:T(8,128)(2,1)} %hidden_ref.1, bf16[1280,2432]{1,0:T(8,128)(2,1)} %head_ref.1, bf16[8,77824]{1,0:T(8,128)(2,1)} %teacher_ref.1, s32[1,256]{1,0:T(1,128)} %bitcast.2, s32[32]{0:T(128)} %teacher_map_hbm.1, ...), custom_call_target="tpu_custom_call" | custom-call | tf_op jit(solution)/shard_map/pallas_call | solution.py:454
  49.7 2.7 %shard_map.86 = (f32[1,256]{1,0:T(1,128)}, bf16[8,1280]{1,0:T(8,128)(2,1)}, bf16[1280,2432]{1,0:T(8,128)(2,1)}) custom-call(f32[1,256]{1,0:T(1,128)S(1)} %get-tuple-element.9.div, bf16[8,1280]{1,0:T(8,128)(2,1)S(1)} %get-tuple-element.10.hgrad, bf16[1280,2432]{1,0:T(8,128)(2,1)S(1)} %get-tuple-element.11.wgrad), custom_call_target="tpu_custom_call" | custom-call | tf_op jit(solution)/shard_map/pallas_call | solution.py:513

commit v4 on v3

--- a/solution.py
+++ b/solution.py
@@ -39,6 +39,7 @@
     hid,
     hid_t,
     grad,
+    head_t,
     diff,
     expo,
     tok_col,
@@ -50,8 +51,7 @@
     hits,
     stat_out,
     stat_in,
-    part_sib,
-    part_own,
+    parts,
     pair_in,
     red_out,
     red_in,
@@ -202,7 +202,7 @@
     def teacher_from(other):
         return remote(staged.at[other], teacher.at[other], t_send.at[0], t_recv.at[other], other)
 
-    for i in range(n - 1):
+    for i in range(10):
         teacher_out(i).start()
 
     teacher[me] = staged[me]
@@ -233,6 +233,16 @@
     )
     norm_mine = top + jnp.log(jnp.sum(gather4(jnp.add, total), axis=1, keepdims=True))
 
+    head_in.wait()
+
+    @pl.loop(0, block // 128)
+    def _(b):
+        at = pl.ds(pl.multiple_of(b * 128, 128), 128)
+        head_t[at, :] = head[:, at].T
+
+    for i in range(10, n - 1):
+        teacher_out(i).start()
+
     for i in range(chips - 1):
         hidden_in(i).wait_recv()
         forward(i).start()
@@ -249,7 +259,6 @@
         forwarded(i).wait_recv()
 
     unpack(1 - core)
-    head_in.wait()
 
     for start, size in tiles(block, 512):
         diff[:, start : start + size] = jnp.dot(
@@ -347,10 +356,6 @@
     final = rows_of([scale, shift, sampled, div])
     columns = jnp.concatenate([final, jnp.zeros((124, tokens), F32)], axis=0).T
     stat[...] = columns
-    halves = columns.reshape(2, chips, rows, 128)
-    ordered = jnp.stack([halves[0], halves[1]], axis=1).reshape(tokens, 128)
-    div_ref[...] = ordered.T[3:4, :]
-
     span = 32
 
     @pl.loop(0, tokens // span)
@@ -371,32 +376,50 @@
     pieces = tiles(width, 256)
 
     def pair(i):
-        return remote(part_sib.at[i], pair_in.at[i], p_send.at[i], p_recv.at[i], sibling)
-
-    for i, (start, size) in enumerate(pieces):
-        part = lax.dot_general(
-            grad[...], head[start : start + size, :], (((1,), (1,)), ((), ())), preferred_element_type=F32
+        return remote(parts.at[i, sib_rows], pair_in.at[i], p_send.at[i], p_recv.at[i], sibling)
+
+    cuts = [(0, 3), (3, len(pieces))]
+
+    def span_of(k):
+        first, last = cuts[k]
+        return slice(pieces[first][0], pieces[last - 1][0] + pieces[last - 1][1])
+
+    def reduce_to(i, k):
+        return remote(
+            red_out.at[chip_to[i], :, span_of(k)], red_in.at[chip, :, span_of(k)],
+            r_send.at[k, i], r_recv.at[k, i], chip_to[i] * 2 + core,
         )
-        stat_rows = jnp.where(core == 0, part[half:], part[:half])
-        part_sib[i] = stat_rows
-        part_own[i] = jnp.where(core == 0, part[:half], part[half:])
-        pair(i).start()
-
-    for i, (start, size) in enumerate(pieces):
-        pair(i).wait_recv()
-        total = part_own[i] + pair_in[i]
-        part_own[i] = total
-        red_out[:, :, start : start + size] = total.reshape(chips, rows, size).astype(BF16)
-
-    def reduce_to(i):
-        return remote(red_out.at[chip_to[i]], red_in.at[chip], r_send.at[i], r_recv.at[i], chip_to[i] * 2 + core)
-
-    def reduce_from(i):
-        return remote(red_out.at[chip], red_in.at[chip_from[i]], r_send.at[i], r_recv.at[i], chip_to[i] * 2 + core)
-
-    for i in range(chips - 1):
-        reduce_to(i).start()
-
+
+    def reduce_from(i, k):
+        return remote(
+            red_out.at[chip, :, span_of(k)], red_in.at[chip_from[i], :, span_of(k)],
+            r_send.at[k, i], r_recv.at[k, i], chip_to[i] * 2 + core,
+        )
+
+    def multiply(k):
+        for i in range(*cuts[k]):
+            start, size = pieces[i]
+            parts[i] = jnp.dot(grad[...], head_t[:, start : start + size], preferred_element_type=F32)
+            pair(i).start()
+
+    def spread_sums(k):
+        for i in range(*cuts[k]):
+            start, size = pieces[i]
+            pair(i).wait_recv()
+            total = parts[i, own_rows] + pair_in[i]
+            parts[i, own_rows] = total
+            red_out[:, :, start : start + size] = total.reshape(chips, rows, size).astype(BF16)
+        for i in range(chips - 1):
+            reduce_to(i, k).start()
+
+    multiply(0)
+    multiply(1)
+    spread_sums(0)
+    spread_sums(1)
+
+    halves = stat[...].reshape(2, chips, rows, 128)
+    ordered = jnp.stack([halves[0], halves[1]], axis=1).reshape(tokens, 128)
+    div_ref[...] = ordered.T[3:4, :]
     red_in[chip] = jnp.zeros((rows, width), BF16)
 
     for start, size in tiles(block, 256):
@@ -405,18 +428,20 @@
         ).astype(BF16)
 
     for i in range(chips - 1):
-        reduce_from(i).wait_recv()
-
-    at = pl.ds(pl.multiple_of(chip * rows, rows), rows)
+        reduce_from(i, 0).wait_recv()
+        reduce_from(i, 1).wait_recv()
+
+    at = pl.ds(pl.multiple_of(my_block * rows, rows), rows)
     for i, (start, size) in enumerate(pieces):
-        total = part_own[i, at, :]
+        total = parts[i, at, :]
         for k in range(chips):
             total = total + red_in[k, :, start : start + size].astype(F32)
         hgrad_ref[:, start : start + size] = total.astype(BF16)
 
     for i in range(chips - 1):
         hidden_out(i).wait_send()
-        reduce_to(i).wait_send()
+        reduce_to(i, 0).wait_send()
+        reduce_to(i, 1).wait_send()
     for i in range(chips):
         forward(i).wait_send()
     for i in range(n - 1):
@@ -472,6 +497,7 @@
             pltpu.VMEM((tokens, width), BF16),
             pltpu.VMEM((width, tokens), BF16),
             pltpu.VMEM((tokens, block), BF16),
+            pltpu.VMEM((block, width), BF16),
             pltpu.VMEM((tokens, block), F32),
             pltpu.VMEM((tokens, block), F32),
             pltpu.VMEM((tokens, 128), F32),
@@ -483,8 +509,7 @@
             pltpu.VMEM((tokens, 128), F32),
             pltpu.VMEM((4, tokens), F32),
             pltpu.VMEM((n, 4, tokens), F32),
-            pltpu.VMEM((pieces, half, 256), F32),
-            pltpu.VMEM((pieces, half, 256), F32),
+            pltpu.VMEM((pieces, tokens, 256), F32),
             pltpu.VMEM((pieces, half, 256), F32),
             pltpu.VMEM((chips, rows, width), BF16),
             pltpu.VMEM((chips, rows, width), BF16),
@@ -500,8 +525,8 @@
             dma((n,)),
             dma((pieces,)),
             dma((pieces,)),
-            dma((chips,)),
-            dma((chips,)),
+            dma((2, chips)),
+            dma((2, chips)),
         ],
         compiler_params=pltpu.CompilerParams(
             collective_id=0, has_side_effects=True, vmem_limit_bytes=48 * 1024 * 1024

time: 52.6 us -> 49.9 us (0.949)
  Pallas kernels: 51.8 us -> 49.2 us
    pallas_call x1, Pallas kernels: 49.1 us -> 46.4 us  [on_device(): pl.pallas_call(functools.partial(kernel, n), out_shape=(pltpu.VMEM((1, to...]
where the time goes in v4:
time: 49.9 us; the launch traced here: 49.8 us
  Pallas kernels  49.2 us (99%)
  between operations  0.64 us (1%)
    pallas_call x1, Pallas kernels, on_device(): pl.pallas_call(functools.partial(kernel, n), out_shape=(pltpu.VMEM((1, to...  46.4 us
    pallas_call x1, Pallas kernels, on_device(): pl.pallas_call(out_kernel, out_shape=(jax.ShapeDtypeStruct((1, tokens), F...  2.74 us

profile of v4, /device:TPU:1, one launch (start us, length us, event | category | flops | bytes accessed | tf_op | source)
XLA Modules:
  0.0 49.8 jit_solution(7197040431969432785)
XLA Ops:
  0.6 46.4 %shard_map.85 = (f32[1,256]{1,0:T(1,128)S(1)}, bf16[8,1280]{1,0:T(8,128)(2,1)S(1)}, bf16[1280,2432]{1,0:T(8,128)(2,1)S(1)}) custom-call(bf16[8,1280]{1,0:T(8,128)(2,1)} %hidden_ref.1, bf16[1280,2432]{1,0:T(8,128)(2,1)} %head_ref.1, bf16[8,77824]{1,0:T(8,128)(2,1)} %teacher_ref.1, s32[1,256]{1,0:T(1,128)} %bitcast.2, s32[32]{0:T(128)} %teacher_map_hbm.1, ...), custom_call_target="tpu_custom_call" | custom-call | tf_op jit(solution)/shard_map/pallas_call | solution.py:479
  47.1 2.7 %shard_map.86 = (f32[1,256]{1,0:T(1,128)}, bf16[8,1280]{1,0:T(8,128)(2,1)}, bf16[1280,2432]{1,0:T(8,128)(2,1)}) custom-call(f32[1,256]{1,0:T(1,128)S(1)} %get-tuple-element.9.div, bf16[8,1280]{1,0:T(8,128)(2,1)S(1)} %get-tuple-element.10.hgrad, bf16[1280,2432]{1,0:T(8,128)(2,1)S(1)} %get-tuple-element.11.wgrad), custom_call_target="tpu_custom_call" | custom-call | tf_op jit(solution)/shard_map/pallas_call | solution.py:538

commit v5 on v4

--- a/solution.py
+++ b/solution.py
@@ -261,18 +261,17 @@
     unpack(1 - core)
 
     for start, size in tiles(block, 512):
-        diff[:, start : start + size] = jnp.dot(
-            hid[...], head[:, start : start + size], preferred_element_type=F32
-        )
+        logits = jnp.dot(hid[...], head[:, start : start + size], preferred_element_type=F32)
+        diff[:, start : start + size] = logits
+        top = functools.reduce(jnp.maximum, [logits[:, c : c + 128] for c in range(0, size, 128)])
+        peaks[...] = top if start == 0 else jnp.maximum(peaks[...], top)
 
     group = 64
 
     @pl.loop(0, tokens // group)
     def _(b):
         at = pl.ds(pl.multiple_of(b * group, group), group)
-        top = diff[at, 0:128]
-        for c in spots[1:]:
-            top = jnp.maximum(top, diff[at, c : c + 128])
+        top = peaks[at, :]
         top = jnp.broadcast_to(jnp.max(top, axis=1, keepdims=True), (group, 128))
         peaks[at, :] = top
         total = jnp.zeros((group, 128), F32)
@@ -290,27 +289,32 @@
     norm_row = norms[...].T[0:1, :]
     lane = lax.broadcasted_iota(jnp.int32, (rows, 128), 1).astype(F32)
 
-    @pl.loop(0, n)
+    @pl.loop(0, chips)
     def _(step):
-        near_y = lax.rem(y + 2 + lax.div(step, 2 * side), side)
-        near_x = lax.rem(x + 2 + lax.div(step, 2), side)
-        other = (near_y * side + near_x) * 2 + lax.rem(step, 2)
-
-        @pl.when(other != me)
-        def _():
-            teacher_from(other).wait_recv()
-
-        at = pl.ds(pl.multiple_of((lax.rem(step, 2) * chips + near_y * side + near_x) * rows, rows), rows)
-        picked = tok_col[at, :] - lane
-        cross = [jnp.zeros((rows, 128), F32)] * 4
-        hit = [jnp.zeros((rows, 128), F32)] * 4
-        for i, c in enumerate(spots):
-            u = diff[at, c : c + 128] - teacher[other, :, c : c + 128].astype(F32)
-            diff[at, c : c + 128] = u
-            cross[i % 4] = cross[i % 4] + expo[at, c : c + 128] * u
-            hit[i % 4] = hit[i % 4] + jnp.where(picked == float(c), u, 0.0)
-        crosses[at, :] = gather4(jnp.add, cross)
-        hits[at, :] = gather4(jnp.add, hit)
+        near_y = lax.rem(y + 2 + lax.div(step, side), side)
+        near_x = lax.rem(x + 2 + step, side)
+        place = near_y * side + near_x
+        for c in range(2):
+            other = place * 2 + c
+
+            @pl.when(other != me)
+            def _():
+                teacher_from(other).wait_recv()
+
+        for c in range(2):
+            other = place * 2 + c
+            at = pl.ds(pl.multiple_of((c * chips + place) * rows, rows), rows)
+            picked = tok_col[at, :] - lane
+            cross = [jnp.zeros((rows, 128), F32)] * 2
+            hit = [jnp.zeros((rows, 128), F32)] * 2
+            for i, spot in enumerate(spots):
+                cols = slice(spot, spot + 128)
+                u = diff[at, cols] - teacher[other, :, cols].astype(F32)
+                diff[at, cols] = u
+                cross[i % 2] = cross[i % 2] + expo[at, cols] * u
+                hit[i % 2] = hit[i % 2] + jnp.where(picked == float(spot), u, 0.0)
+            crosses[at, :] = cross[0] + cross[1]
+            hits[at, :] = hit[0] + hit[1]
 
     row = lax.broadcasted_iota(jnp.int32, (4, tokens), 0)
 

time: 49.9 us -> 49.8 us (level)
  no operation moved by 1% of the time
where the time goes in v5:
time: 49.8 us; the launch traced here: 49.7 us
  Pallas kernels  49.1 us (99%)
  between operations  0.64 us (1%)
    pallas_call x1, Pallas kernels, on_device(): pl.pallas_call(functools.partial(kernel, n), out_shape=(pltpu.VMEM((1, to...  46.3 us
    pallas_call x1, Pallas kernels, on_device(): pl.pallas_call(out_kernel, out_shape=(jax.ShapeDtypeStruct((1, tokens), F...  2.74 us

profile of v5, /device:TPU:1, one launch (start us, length us, event | category | flops | bytes accessed | tf_op | source)
XLA Modules:
  0.0 49.7 jit_solution(2926353852539587055)
XLA Ops:
  0.6 46.3 %shard_map.85 = (f32[1,256]{1,0:T(1,128)S(1)}, bf16[8,1280]{1,0:T(8,128)(2,1)S(1)}, bf16[1280,2432]{1,0:T(8,128)(2,1)S(1)}) custom-call(bf16[8,1280]{1,0:T(8,128)(2,1)} %hidden_ref.1, bf16[1280,2432]{1,0:T(8,128)(2,1)} %head_ref.1, bf16[8,77824]{1,0:T(8,128)(2,1)} %teacher_ref.1, s32[1,256]{1,0:T(1,128)} %bitcast.2, s32[32]{0:T(128)} %teacher_map_hbm.1, ...), custom_call_target="tpu_custom_call" | custom-call | tf_op jit(solution)/shard_map/pallas_call | solution.py:483
  47.0 2.7 %shard_map.86 = (f32[1,256]{1,0:T(1,128)}, bf16[8,1280]{1,0:T(8,128)(2,1)}, bf16[1280,2432]{1,0:T(8,128)(2,1)}) custom-call(f32[1,256]{1,0:T(1,128)S(1)} %get-tuple-element.9.div, bf16[8,1280]{1,0:T(8,128)(2,1)S(1)} %get-tuple-element.10.hgrad, bf16[1280,2432]{1,0:T(8,128)(2,1)S(1)} %get-tuple-element.11.wgrad), custom_call_target="tpu_custom_call" | custom-call | tf_op jit(solution)/shard_map/pallas_call | solution.py:542
